TPU v7x, 512 devices: a whole 4x8x8 slice. The times are simulated.
512 devices in a mesh: dp: 4 (over x), row: 16 (over y, core), col: 8 (over z).
Axes of the slice: x: 4, y: 8, z: 8, core: 2. Of those that a mesh axis runs over, the one named last changes fastest.
Arguments:
- grad_wi: bfloat16 [4, 4096, 16384], P('dp', 'row', 'col'), may hold values from -100 to 100
- grad_wo: bfloat16 [4, 16384, 4096], P('dp', 'row', 'col'), may hold values from -100 to 100
- row_wi: float32 [4096], P('row'), may hold values from 0.01 to 1
- col_wi: float32 [16384], P('col'), may hold values from 0.01 to 1
- row_wo: float32 [16384], P('row'), may hold values from 0.01 to 1
- col_wo: float32 [4096], P('col'), may hold values from 0.01 to 1
Outputs:
- update_wi: bfloat16 [4096, 16384], P('row', 'col')
- row_wi_new: float32 [4096], P('row')
- col_wi_new: float32 [16384], P('col')
- update_wo: bfloat16 [16384, 4096], P('row', 'col')
- row_wo_new: float32 [16384], P('row')
- col_wo_new: float32 [4096], P('col')
All inputs are finite; a program needn't handle non-finite values.
Results may differ from a plain program's by a relative error of at most 0.015.
Values may be sent and summed in bfloat16 or wider, within the bound.
A program may use at most 64 MiB of HBM per device.

v0:
```python
import jax
import jax.numpy as jnp
from jax import lax
from jax.sharding import PartitionSpec as P

D = 4096
FF = 16384
BETA = 0.8
EPS_SQUARE = 1e-30


def column_totals(square_wi, square_wo):
    return lax.psum((jnp.sum(square_wi, axis=0), jnp.sum(square_wo, axis=0)), "row")


def local(grad_wi, grad_wo, row_wi, col_wi, row_wo, col_wo):
    terms = (grad_wi[0].astype(jnp.float32), grad_wo[0].astype(jnp.float32))
    total_wi, total_wo = (
        lax.psum(terms[0].astype(jnp.bfloat16), "dp").astype(jnp.float32),
        lax.psum(terms[1].astype(jnp.bfloat16), "dp").astype(jnp.float32),
    )
    square_wi = total_wi * total_wi + EPS_SQUARE
    square_wo = total_wo * total_wo + EPS_SQUARE
    row_sum_wi, row_sum_wo = lax.psum(
        (jnp.sum(square_wi, axis=1), jnp.sum(square_wo, axis=1)), "col"
    )
    col_sum_wi, col_sum_wo = column_totals(square_wi, square_wo)
    row_new_wi = BETA * row_wi + (1.0 - BETA) * (row_sum_wi / FF)
    row_new_wo = BETA * row_wo + (1.0 - BETA) * (row_sum_wo / D)
    col_new_wi = BETA * col_wi + (1.0 - BETA) * (col_sum_wi / D)
    col_new_wo = BETA * col_wo + (1.0 - BETA) * (col_sum_wo / FF)
    raw_wi = total_wi / jnp.sqrt(row_new_wi[:, None] * col_new_wi[None, :])
    raw_wo = total_wo / jnp.sqrt(row_new_wo[:, None] * col_new_wo[None, :])
    local_squares = (jnp.sum(raw_wi * raw_wi), jnp.sum(raw_wo * raw_wo))
    energy_wi, energy_wo = lax.psum((local_squares[0], local_squares[1]), ("row", "col"))
    update_wi = (raw_wi / jnp.maximum(1.0, jnp.sqrt(energy_wi / (D * FF)))).astype(jnp.bfloat16)
    update_wo = (raw_wo / jnp.maximum(1.0, jnp.sqrt(energy_wo / (D * FF)))).astype(jnp.bfloat16)
    return (update_wi, row_new_wi, col_new_wi, update_wo, row_new_wo, col_new_wo)


def solution(mesh):
    return jax.shard_map(
        local,
        mesh=mesh,
        in_specs=(
            P("dp", "row", "col"),
            P("dp", "row", "col"),
            P("row"),
            P("col"),
            P("row"),
            P("col"),
        ),
        out_specs=(P("row", "col"), P("row"), P("col"), P("row", "col"), P("row"), P("col")),
        check_vma=False,
    )
```

profile of v0, /device:TPU:64, one launch (start us, length us, event | category | flops | bytes accessed | tf_op | source)
XLA Modules:
  0.0 412.7 jit_solution(8415651941492895730)
XLA Ops:
  7.2 0.0 all-reduce.6.cloned.1.call-start
  7.2 0.7 all-reduce.6.cloned.1.call-update
  7.9 76.1 %all-reduce.6.cloned.1.call-done = (bf16[256,2048]{1,0:T(8,128)(2,1)}, bf16[1024,512]{1,0:T(8,128)(2,1)}) async-done(((bf16[256,2048]{1,0:T(8,128)(2,1)}, bf16[1024,512]{1,0:T(8,128)(2,1)}), (bf16[256,2048]{1,0:T(8,128)(2,1)}, bf16[1024,512]{1,0:T(8,128)(2,1)})) %all-reduce.6.cloned.1.call-update) | async-done | bytes 2097168 | tf_op jit(solution)/shard_map/psum | solution.py:19
  84.0 0.0 copy-start.1
  84.0 0.0 copy-start.9
  84.0 0.0 copy-start.7
  84.0 0.0 copy-start.6
  84.0 1.8 fusion.5
  85.8 0.0 copy-done.1
  85.8 0.0 copy-start.8
  85.8 0.0 copy-start
  85.8 0.5 fusion.2
  86.3 16.8 %all-reduce.2 = (f32[256]{0:T(256)S(1)}, f32[1024]{0:T(1024)S(1)}) all-reduce(f32[256]{0:T(256)S(1)} %get-tuple-element.8, f32[1024]{0:T(1024)S(1)} %get-tuple-element.6), channel_id=1, replica_groups=mesh['dp'=4,'row'=16,'col'=8] {'col'}, use_global_device_ids=true, to_apply=%region_2.0 | all-reduce | flops 1280 | bytes 10240 | tf_op jit(solution)/shard_map/psum | solution.py:24
  103.1 0.0 copy-done.9
  103.1 0.0 copy-start.5
  103.1 0.0 copy-done.7
  103.1 0.0 copy-start.3
  103.2 45.7 %all-reduce.1 = (f32[2048]{0:T(1024)S(1)}, f32[512]{0:T(512)S(1)}) all-reduce(f32[2048]{0:T(1024)S(1)} %get-tuple-element.9, f32[512]{0:T(512)S(1)} %get-tuple-element.7), channel_id=1, replica_groups=mesh['dp'=4,'row'=16,'col'=8] {'row'}, use_global_device_ids=true, to_apply=%region_4.0 | all-reduce | flops 2560 | bytes 20480 | tf_op jit(solution)/shard_map/psum | solution.py:13
  148.9 0.0 copy-done.6
  148.9 0.0 copy-start.2
  148.9 1.5 multiply_reduce_fusion.1
  150.4 0.0 copy-done.8
  150.4 0.0 copy-done
  150.4 0.0 copy-start.4
  150.4 1.4 multiply_reduce_fusion
  151.9 249.7 %all-reduce = (f32[]{:T(128)}, f32[]{:T(128)}) all-reduce(f32[]{:T(128)} %multiply_reduce_fusion.1, f32[]{:T(128)} %multiply_reduce_fusion), channel_id=1, replica_groups=mesh['dp'=4,'row'=16,'col'=8] {'row','col'}, use_global_device_ids=true, to_apply=%region_6.0 | all-reduce | flops 2 | bytes 16 | tf_op jit(solution)/shard_map/psum | solution.py:35
  403.0 0.0 copy-done.5
  403.0 0.0 copy-done.2
  403.0 1.4 divide_convert_fusion.1
  404.4 0.0 copy-done.3
  404.4 0.0 copy-done.4
  404.4 1.4 divide_convert_fusion
  (4 shorter events, 0.0 us)
Async XLA Ops:
  7.2 76.8 %all-reduce.6.cloned.1.call-start = ((), (), s32[]{:S(2)}) async-start(), calls=%async_computation | async-start | bytes 4194304 | tf_op jit(solution)/shard_map/psum | solution.py:19
  84.0 1.8 copy-start.1
  84.0 19.1 %copy-start.9 = (f32[256]{0:T(256)S(1)}, f32[256]{0:T(256)}, u32[]{:S(2)}) copy-start(f32[256]{0:T(256)} %param.8) | copy-start | bytes 3076
  84.0 19.1 %copy-start.7 = (f32[1024]{0:T(1024)S(1)}, f32[1024]{0:T(1024)}, u32[]{:S(2)}) copy-start(f32[1024]{0:T(1024)} %param.10) | copy-start | bytes 12292
  84.0 64.9 %copy-start.6 = (f32[2048]{0:T(1024)S(1)}, f32[2048]{0:T(1024)}, u32[]{:S(2)}) copy-start(f32[2048]{0:T(1024)} %param.9) | copy-start | bytes 24580
  85.8 64.6 %copy-start.8 = (f32[512]{0:T(512)S(1)}, f32[512]{0:T(512)}, u32[]{:S(2)}) copy-start(f32[512]{0:T(512)} %param.11) | copy-start | bytes 6148
  85.8 64.6 %copy-start = (bf16[1024,512]{1,0:T(8,128)(2,1)S(1)}, bf16[1024,512]{1,0:T(8,128)(2,1)}, u32[]{:S(2)}) copy-start(bf16[1024,512]{1,0:T(8,128)(2,1)} %get-tuple-element.17) | copy-start | bytes 3145732
  103.1 299.9 %copy-start.5 = (f32[256]{0:T(256)}, f32[256]{0:T(256)S(1)}, u32[]{:S(2)}) copy-start(f32[256]{0:T(256)S(1)} %multiply_add_fusion.3) | copy-start | bytes 3076
  103.1 301.3 %copy-start.3 = (f32[1024]{0:T(1024)}, f32[1024]{0:T(1024)S(1)}, u32[]{:S(2)}) copy-start(f32[1024]{0:T(1024)S(1)} %multiply_add_fusion.1) | copy-start | bytes 12292
  148.9 254.1 %copy-start.2 = (f32[2048]{0:T(1024)}, f32[2048]{0:T(1024)S(1)}, u32[]{:S(2)}) copy-start(f32[2048]{0:T(1024)S(1)} %multiply_add_fusion) | copy-start | bytes 24580
  150.4 254.0 %copy-start.4 = (f32[512]{0:T(512)}, f32[512]{0:T(512)S(1)}, u32[]{:S(2)}) copy-start(f32[512]{0:T(512)S(1)} %multiply_add_fusion.2) | copy-start | bytes 6148
Sparse Core Ops, SparseCore 0:
  10.4 73.4 all-reduce.5
where the time goes:
time: 413 us
  blocking collectives  312 us (76%)
  waiting for transfers between devices  76.8 us (19%)
  between operations  15.5 us (4%)
  other arithmetic  8.11 us (2%)
    psum x1, blocking collectives, local(): lax.psum((local_squares[0], local_squares[1]), ('row', 'col'))  250 us
    psum x1, waiting for transfers between devices, local(): lax.psum(terms[0].astype(jnp.bfloat16), 'dp').astype(jnp.float32)  76.1 us
    psum x1, blocking collectives, column_totals(): lax.psum((jnp.sum(square_wi, axis=0), jnp.sum(square_wo, axis=0)), 'row')  45.7 us
    psum x1, blocking collectives, local(): lax.psum((jnp.sum(square_wi, axis=1), jnp.sum(square_wo, axis=1)), 'col')  16.8 us
  transfers between devices with their start and end apart: 1, of which 1 were waited for; matrix products, arithmetic and copies ran while one was open for 0% of the time, Pallas kernels for 0%

commit v1 on v0

--- a/solution.py
+++ b/solution.py
@@ -1,3 +1,4 @@
+import functools
 import jax
 import jax.numpy as jnp
 from jax import lax
@@ -7,6 +8,15 @@
 FF = 16384
 BETA = 0.8
 EPS_SQUARE = 1e-30
+
+
+def show_state(frame, device_axis, row_axis):
+    for h in (device_axis, row_axis):
+        frame = jax.lax.psum(frame, axis_name=h)
+    return frame
+
+
+_render_floor = functools.partial(show_state, device_axis="col", row_axis="row")
 
 
 def column_totals(square_wi, square_wo):
@@ -32,7 +42,7 @@
     raw_wi = total_wi / jnp.sqrt(row_new_wi[:, None] * col_new_wi[None, :])
     raw_wo = total_wo / jnp.sqrt(row_new_wo[:, None] * col_new_wo[None, :])
     local_squares = (jnp.sum(raw_wi * raw_wi), jnp.sum(raw_wo * raw_wo))
-    energy_wi, energy_wo = lax.psum((local_squares[0], local_squares[1]), ("row", "col"))
+    energy_wi, energy_wo = _render_floor((local_squares[0], local_squares[1]))
     update_wi = (raw_wi / jnp.maximum(1.0, jnp.sqrt(energy_wi / (D * FF)))).astype(jnp.bfloat16)
     update_wo = (raw_wo / jnp.maximum(1.0, jnp.sqrt(energy_wo / (D * FF)))).astype(jnp.bfloat16)
     return (update_wi, row_new_wi, col_new_wi, update_wo, row_new_wo, col_new_wo)

time: 413 us -> 206 us (0.50)
  the two profiles are of different devices: /device:TPU:64 before, /device:TPU:1 now
where the time goes in v1:
time: 206 us
  blocking collectives  104 us (50%)
  waiting for transfers between devices  78.3 us (38%)
  between operations  15.5 us (8%)
  other arithmetic  8.11 us (4%)
    psum x1, waiting for transfers between devices, local(): lax.psum(terms[0].astype(jnp.bfloat16), 'dp').astype(jnp.float32)  77.6 us
    psum x1, blocking collectives, column_totals(): lax.psum((jnp.sum(square_wi, axis=0), jnp.sum(square_wo, axis=0)), 'row')  46.7 us
    psum x2, blocking collectives, show_state(): frame = jax.lax.psum(frame, axis_name=h)  42.4 us
    psum x1, blocking collectives, local(): lax.psum((jnp.sum(square_wi, axis=1), jnp.sum(square_wo, axis=1)), 'col')  14.6 us
  transfers between devices with their start and end apart: 1, of which 1 were waited for; matrix products, arithmetic and copies ran while one was open for 0% of the time, Pallas kernels for 0%

profile of v1, /device:TPU:1, one launch (start us, length us, event | category | flops | bytes accessed | tf_op | source)
XLA Modules:
  0.0 205.7 jit_solution(5595017636434755267)
XLA Ops:
  7.2 0.0 all-reduce.7.cloned.1.call-start
  7.2 0.7 all-reduce.7.cloned.1.call-update
  7.9 77.6 %all-reduce.7.cloned.1.call-done = (bf16[256,2048]{1,0:T(8,128)(2,1)}, bf16[1024,512]{1,0:T(8,128)(2,1)}) async-done(((bf16[256,2048]{1,0:T(8,128)(2,1)}, bf16[1024,512]{1,0:T(8,128)(2,1)}), (bf16[256,2048]{1,0:T(8,128)(2,1)}, bf16[1024,512]{1,0:T(8,128)(2,1)})) %all-reduce.7.cloned.1.call-update) | async-done | bytes 2097168 | tf_op jit(solution)/shard_map/psum | solution.py:29
  85.5 0.0 copy-start.1
  85.5 0.0 copy-start.9
  85.5 0.0 copy-start.7
  85.5 0.0 copy-start.6
  85.5 1.8 fusion.5
  87.3 0.0 copy-done.1
  87.3 0.0 copy-start.8
  87.3 0.0 copy-start
  87.4 0.5 fusion.2
  87.9 14.6 %all-reduce.3 = (f32[256]{0:T(256)S(1)}, f32[1024]{0:T(1024)S(1)}) all-reduce(f32[256]{0:T(256)S(1)} %get-tuple-element.8, f32[1024]{0:T(1024)S(1)} %get-tuple-element.6), channel_id=1, replica_groups=mesh['dp'=4,'row'=16,'col'=8] {'col'}, use_global_device_ids=true, to_apply=%region_2.0 | all-reduce | flops 1280 | bytes 10240 | tf_op jit(solution)/shard_map/psum | solution.py:34
  102.5 0.0 copy-done.9
  102.5 0.0 copy-start.5
  102.5 0.0 copy-done.7
  102.5 0.0 copy-start.3
  102.5 46.7 %all-reduce.1 = (f32[2048]{0:T(1024)S(1)}, f32[512]{0:T(512)S(1)}) all-reduce(f32[2048]{0:T(1024)S(1)} %get-tuple-element.9, f32[512]{0:T(512)S(1)} %get-tuple-element.7), channel_id=1, replica_groups=mesh['dp'=4,'row'=16,'col'=8] {'row'}, use_global_device_ids=true, to_apply=%region_4.0 | all-reduce | flops 2560 | bytes 20480 | tf_op jit(solution)/shard_map/psum | solution.py:23
  149.2 0.0 copy-done.6
  149.2 1.5 multiply_reduce_fusion.1
  150.7 0.0 copy-done.8
  150.7 0.0 copy-done
  150.7 0.0 copy-start.4
  150.8 1.4 multiply_reduce_fusion
  152.2 11.6 %all-reduce.2 = (f32[]{:T(128)}, f32[]{:T(128)}) all-reduce(f32[]{:T(128)} %multiply_reduce_fusion.1, f32[]{:T(128)} %multiply_reduce_fusion), channel_id=1, replica_groups=mesh['dp'=4,'row'=16,'col'=8] {'col'}, use_global_device_ids=true, to_apply=%region_6.0 | all-reduce | flops 2 | bytes 16 | tf_op jit(solution)/shard_map/psum | solution.py:15
  163.7 30.8 %all-reduce = (f32[]{:T(128)}, f32[]{:T(128)}) all-reduce(f32[]{:T(128)} %get-tuple-element.14, f32[]{:T(128)} %get-tuple-element.15), channel_id=1, replica_groups=mesh['dp'=4,'row'=16,'col'=8] {'row'}, use_global_device_ids=true, to_apply=%region_7.0 | all-reduce | flops 2 | bytes 16 | tf_op jit(solution)/shard_map/psum | solution.py:15
  195.9 0.0 copy-done.5
  196.0 0.0 copy-done.2
  196.0 1.4 divide_convert_fusion.1
  197.4 0.0 copy-done.3
  197.4 0.0 copy-done.4
  197.4 1.4 divide_convert_fusion
  (5 shorter events, 0.0 us)
Async XLA Ops:
  7.2 78.4 %all-reduce.7.cloned.1.call-start = ((), (), s32[]{:S(2)}) async-start(), calls=%async_computation | async-start | bytes 4194304 | tf_op jit(solution)/shard_map/psum | solution.py:29
  85.5 1.8 copy-start.1
  85.5 16.9 %copy-start.9 = (f32[256]{0:T(256)S(1)}, f32[256]{0:T(256)}, u32[]{:S(2)}) copy-start(f32[256]{0:T(256)} %param.8) | copy-start | bytes 3076
  85.5 17.0 %copy-start.7 = (f32[1024]{0:T(1024)S(1)}, f32[1024]{0:T(1024)}, u32[]{:S(2)}) copy-start(f32[1024]{0:T(1024)} %param.10) | copy-start | bytes 12292
  85.5 63.7 %copy-start.6 = (f32[2048]{0:T(1024)S(1)}, f32[2048]{0:T(1024)}, u32[]{:S(2)}) copy-start(f32[2048]{0:T(1024)} %param.9) | copy-start | bytes 24580
  87.3 63.4 %copy-start.8 = (f32[512]{0:T(512)S(1)}, f32[512]{0:T(512)}, u32[]{:S(2)}) copy-start(f32[512]{0:T(512)} %param.11) | copy-start | bytes 6148
  87.3 63.4 %copy-start = (bf16[1024,512]{1,0:T(8,128)(2,1)S(1)}, bf16[1024,512]{1,0:T(8,128)(2,1)}, u32[]{:S(2)}) copy-start(bf16[1024,512]{1,0:T(8,128)(2,1)} %get-tuple-element.19) | copy-start | bytes 3145732
  102.5 93.5 %copy-start.5 = (f32[256]{0:T(256)}, f32[256]{0:T(256)S(1)}, u32[]{:S(2)}) copy-start(f32[256]{0:T(256)S(1)} %multiply_add_fusion.3) | copy-start | bytes 3076
  102.5 94.9 %copy-start.3 = (f32[1024]{0:T(1024)}, f32[1024]{0:T(1024)S(1)}, u32[]{:S(2)}) copy-start(f32[1024]{0:T(1024)S(1)} %multiply_add_fusion.1) | copy-start | bytes 12292
  149.2 46.8 %copy-start.2 = (f32[2048]{0:T(1024)}, f32[2048]{0:T(1024)S(1)}, u32[]{:S(2)}) copy-start(f32[2048]{0:T(1024)S(1)} %multiply_add_fusion) | copy-start | bytes 24580
  150.7 46.6 %copy-start.4 = (f32[512]{0:T(512)}, f32[512]{0:T(512)S(1)}, u32[]{:S(2)}) copy-start(f32[512]{0:T(512)S(1)} %multiply_add_fusion.2) | copy-start | bytes 6148
Sparse Core Ops, SparseCore 0:
  10.4 75.0 all-reduce.6

commit v2 on v0

--- a/solution.py
+++ b/solution.py
@@ -9,6 +9,10 @@
 EPS_SQUARE = 1e-30
 
 
+def lift_waves(incoming_x):
+    return jnp.sum(lax.all_gather(incoming_x, axis_name="dp"), axis=0)
+
+
 def column_totals(square_wi, square_wo):
     return lax.psum((jnp.sum(square_wi, axis=0), jnp.sum(square_wo, axis=0)), "row")
 
@@ -16,7 +20,7 @@
 def local(grad_wi, grad_wo, row_wi, col_wi, row_wo, col_wo):
     terms = (grad_wi[0].astype(jnp.float32), grad_wo[0].astype(jnp.float32))
     total_wi, total_wo = (
-        lax.psum(terms[0].astype(jnp.bfloat16), "dp").astype(jnp.float32),
+        lift_waves(terms[0].astype(jnp.bfloat16)).astype(jnp.float32),
         lax.psum(terms[1].astype(jnp.bfloat16), "dp").astype(jnp.float32),
     )
     square_wi = total_wi * total_wi + EPS_SQUARE

time: 413 us -> 458 us (1.11)
  waiting for transfers between devices: 76.8 us -> 119 us
    all_gather x0 -> x1, waiting for transfers between devices: none -> 55.1 us  [lift_waves(): return jnp.sum(lax.all_gather(incoming_x, axis_name='dp'), axis=0)]
    psum x1, waiting for transfers between devices: 76.1 us -> 62.2 us  [local(): lax.psum(terms[1].astype(jnp.bfloat16), 'dp').astype(jnp.float32)]
  transfers between devices with their start and end apart: 1 -> 2, of which waited for: 1 -> 2; matrix products, arithmetic and copies ran while one was open for 0% -> 0% of each run, Pallas kernels for 0% -> 0%
where the time goes in v2:
time: 458 us
  blocking collectives  312 us (68%)
  waiting for transfers between devices  119 us (26%)
  between operations  15.5 us (3%)
  other arithmetic  11.1 us (2%)
    psum x1, blocking collectives, local(): lax.psum((local_squares[0], local_squares[1]), ('row', 'col'))  250 us
    psum x1, waiting for transfers between devices, local(): lax.psum(terms[1].astype(jnp.bfloat16), 'dp').astype(jnp.float32)  62.2 us
    all_gather x1, waiting for transfers between devices, lift_waves(): return jnp.sum(lax.all_gather(incoming_x, axis_name='dp'), axis=0)  55.1 us
    psum x1, blocking collectives, column_totals(): lax.psum((jnp.sum(square_wi, axis=0), jnp.sum(square_wo, axis=0)), 'row')  45.7 us
    psum x1, blocking collectives, local(): lax.psum((jnp.sum(square_wi, axis=1), jnp.sum(square_wo, axis=1)), 'col')  16.8 us
  transfers between devices with their start and end apart: 2, of which 2 were waited for; matrix products, arithmetic and copies ran while one was open for 0% of the time, Pallas kernels for 0%

profile of v2, /device:TPU:64, one launch (start us, length us, event | category | flops | bytes accessed | tf_op | source)
XLA Modules:
  0.0 457.6 jit_solution(3350081097873036498)
XLA Ops:
  7.2 0.0 all-reduce.5.cloned.1.call-start
  7.2 0.7 all-reduce.5.cloned.1.call-update
  7.9 0.0 all-gather.2.cloned.1.call-start
  7.9 0.7 all-gather.2.cloned.1.call-update
  8.6 62.2 %all-reduce.5.cloned.1.call-done = bf16[1024,512]{1,0:T(8,128)(2,1)} async-done(((bf16[1024,512]{1,0:T(8,128)(2,1)}), bf16[1024,512]{1,0:T(8,128)(2,1)}) %all-reduce.5.cloned.1.call-update) | async-done | bytes 1048592 | tf_op jit(solution)/shard_map/psum | solution.py:24
  70.8 1.7 fusion.5
  72.5 0.0 copy-start.8
  72.5 0.0 copy-start.5
  72.5 55.1 %all-gather.2.cloned.1.call-done = bf16[4,256,2048]{2,1,0:T(8,128)(2,1)} async-done(((bf16[1,256,2048]{2,1,0:T(8,128)(2,1)}), bf16[4,256,2048]{2,1,0:T(8,128)(2,1)}) %all-gather.2.cloned.1.call-update) | async-done | bytes 4194320 | tf_op jit(solution)/shard_map/all_gather | solution.py:13
  127.7 3.1 reduce_sum.66
  130.8 0.0 copy-start.7
  130.8 0.0 copy-start.6
  130.8 0.0 copy-start
  130.8 0.5 fusion.2
  131.3 16.8 %all-reduce.2 = (f32[256]{0:T(256)S(1)}, f32[1024]{0:T(1024)S(1)}) all-reduce(f32[256]{0:T(256)S(1)} %get-tuple-element.8, f32[1024]{0:T(1024)S(1)} %get-tuple-element.6), channel_id=1, replica_groups=mesh['dp'=4,'row'=16,'col'=8] {'col'}, use_global_device_ids=true, to_apply=%region_2.0 | all-reduce | flops 1280 | bytes 10240 | tf_op jit(solution)/shard_map/psum | solution.py:28
  148.1 0.0 copy-done.8
  148.1 0.0 copy-start.4
  148.1 45.7 %all-reduce.1 = (f32[2048]{0:T(1024)S(1)}, f32[512]{0:T(512)S(1)}) all-reduce(f32[2048]{0:T(1024)S(1)} %get-tuple-element.9, f32[512]{0:T(512)S(1)} %get-tuple-element.7), channel_id=1, replica_groups=mesh['dp'=4,'row'=16,'col'=8] {'row'}, use_global_device_ids=true, to_apply=%region_4.0 | all-reduce | flops 2560 | bytes 20480 | tf_op jit(solution)/shard_map/psum | solution.py:17
  193.8 0.0 copy-done.5
  193.8 1.5 multiply_reduce_fusion.1
  195.3 0.0 copy-done.7
  195.4 0.0 copy-done.6
  195.4 0.0 copy-done
  195.4 0.0 copy-start.2
  195.4 1.4 multiply_reduce_fusion
  196.8 249.7 %all-reduce = (f32[]{:T(128)}, f32[]{:T(128)}) all-reduce(f32[]{:T(128)} %multiply_reduce_fusion.1, f32[]{:T(128)} %multiply_reduce_fusion), channel_id=1, replica_groups=mesh['dp'=4,'row'=16,'col'=8] {'row','col'}, use_global_device_ids=true, to_apply=%region_6.0 | all-reduce | flops 2 | bytes 16 | tf_op jit(solution)/shard_map/psum | solution.py:39
  447.9 1.4 divide_convert_fusion.1
  449.4 0.0 copy-done.4
  449.4 0.0 copy-done.1
  449.4 1.4 divide_convert_fusion
  450.8 0.0 copy-done.3
  450.8 0.0 copy-done.2
  (6 shorter events, 0.0 us)
Async XLA Ops:
  7.2 63.7 %all-reduce.5.cloned.1.call-start = ((), (), s32[]{:S(2)}) async-start(), calls=%async_computation.1 | async-start | bytes 2097152 | tf_op jit(solution)/shard_map/psum | solution.py:24
  7.9 119.8 %all-gather.2.cloned.1.call-start = ((), (), s32[]{:S(2)}) async-start(), calls=%async_computation | async-start | bytes 5242880 | tf_op jit(solution)/shard_map/all_gather | solution.py:13
  72.5 75.5 %copy-start.8 = (f32[256]{0:T(256)S(1)}, f32[256]{0:T(256)}, u32[]{:S(2)}) copy-start(f32[256]{0:T(256)} %param.8) | copy-start | bytes 3076
  72.5 121.3 %copy-start.5 = (f32[2048]{0:T(1024)S(1)}, f32[2048]{0:T(1024)}, u32[]{:S(2)}) copy-start(f32[2048]{0:T(1024)} %param.9) | copy-start | bytes 24580
  130.8 64.6 %copy-start.7 = (f32[512]{0:T(512)S(1)}, f32[512]{0:T(512)}, u32[]{:S(2)}) copy-start(f32[512]{0:T(512)} %param.11) | copy-start | bytes 6148
  130.8 64.6 %copy-start.6 = (f32[1024]{0:T(1024)S(1)}, f32[1024]{0:T(1024)}, u32[]{:S(2)}) copy-start(f32[1024]{0:T(1024)} %param.10) | copy-start | bytes 12292
  130.8 64.6 %copy-start = (bf16[1024,512]{1,0:T(8,128)(2,1)S(1)}, bf16[1024,512]{1,0:T(8,128)(2,1)}, u32[]{:S(2)}) copy-start(bf16[1024,512]{1,0:T(8,128)(2,1)} %all-reduce.5.cloned.1.call-done) | copy-start | bytes 3145732
  148.1 301.3 %copy-start.4 = (f32[256]{0:T(256)}, f32[256]{0:T(256)S(1)}, u32[]{:S(2)}) copy-start(f32[256]{0:T(256)S(1)} %multiply_add_fusion.3) | copy-start | bytes 3076
  193.8 255.5 %copy-start.1 = (f32[2048]{0:T(1024)}, f32[2048]{0:T(1024)S(1)}, u32[]{:S(2)}) copy-start(f32[2048]{0:T(1024)S(1)} %multiply_add_fusion) | copy-start | bytes 24580
  195.4 255.4 %copy-start.3 = (f32[512]{0:T(512)}, f32[512]{0:T(512)S(1)}, u32[]{:S(2)}) copy-start(f32[512]{0:T(512)S(1)} %multiply_add_fusion.2) | copy-start | bytes 6148
  195.4 255.4 %copy-start.2 = (f32[1024]{0:T(1024)}, f32[1024]{0:T(1024)S(1)}, u32[]{:S(2)}) copy-start(f32[1024]{0:T(1024)S(1)} %multiply_add_fusion.1) | copy-start | bytes 12292
Sparse Core Ops, SparseCore 0:
  10.4 60.4 all-reduce.4
  73.1 54.4 all-gather.1
